TPU v7x, 32 devices: a whole 2x2x4 slice. The times are simulated.
32 devices in a mesh: section: 4 (over x, core), seq: 8 (over z, y).
Axes of the slice: x: 2, y: 2, z: 4, core: 2. Of those that a mesh axis runs over, the one named last changes fastest.
Arguments:
- q_img: bfloat16 [1024, 3072], P('seq', 'section'), may hold values from -6 to 6
- k_img: bfloat16 [1024, 3072], P('seq', 'section'), may hold values from -6 to 6
- v_img: bfloat16 [1024, 3072], P('seq', 'section'), may hold values from -6 to 6
- q_txt: bfloat16 [256, 3072], P('seq', 'section'), may hold values from -6 to 6
- k_txt: bfloat16 [256, 3072], P('seq', 'section'), may hold values from -6 to 6
- v_txt: bfloat16 [256, 3072], P('seq', 'section'), may hold values from -6 to 6
- norm_gains: float32 [4, 128], replicated, may hold values from 1.2 to 2
- block_map: int32 [24, 8, 8], P('section', 'seq'), may hold values 0 or 1
Outputs:
- image_out: bfloat16 [256, 4, 3072], P('seq', 'section')
- text_out: bfloat16 [256, 3072], P('seq', 'section')
All inputs are finite; a program needn't handle non-finite values. No bound on the sum of `block_map` on one device may be relied on, other than what follows from the above.
Results may differ from a plain program's by a relative error of at most 0.011.
Values may be sent and summed in bfloat16 or wider, within the bound.
A program may use at most 256 MiB of HBM per device.

v0:
```python
import jax
import jax.numpy as jnp
from jax import lax
from jax.sharding import PartitionSpec as P

BLOCK = 128


def normed(values, gain, heads):
    rows = values.shape[0]
    floats = values.astype(jnp.float32).reshape(rows, heads, gain.shape[0])
    power = jnp.mean(floats * floats, axis=-1, keepdims=True)
    return (floats * lax.rsqrt(power + 1e-06) * gain).astype(jnp.bfloat16)


def make_keep(flags, query_shards, shards, first, rows, text_rows):
    heads = flags.shape[0]
    key_blocks = rows // BLOCK
    stride = rows + text_rows
    picked = lax.dynamic_slice_in_dim(flags, first * key_blocks, shards * key_blocks, 2)
    picked = picked.reshape(heads, query_shards, key_blocks, shards, key_blocks)
    image_mask = jnp.broadcast_to(
        picked[:, :, :, None, :, :, None] > 0,
        (heads, query_shards, key_blocks, BLOCK, shards, key_blocks, BLOCK),
    )
    image_mask = image_mask.reshape(heads, query_shards, rows, shards, rows)
    keep = jnp.pad(
        image_mask, ((0, 0), (0, 0), (0, text_rows), (0, 0), (0, text_rows)), constant_values=True
    )
    return keep.reshape(heads, query_shards * stride, shards, stride)


def accumulate(queries, flags, query_shards, rows, text_rows, carry, pieces, start):
    numer, denom = carry
    piece_keys, piece_values = pieces
    heads = queries.shape[1]
    head_size = queries.shape[2]
    stride = rows + text_rows
    shards = piece_keys.shape[0] // stride
    first = start // stride
    keys_four = piece_keys.reshape(shards, stride, heads, head_size)
    values_four = piece_values.reshape(shards, stride, heads, head_size)
    scores = jnp.einsum(
        "qhd,skhd->hqsk", queries, keys_four, preferred_element_type=jnp.float32
    ) * head_size ** (-0.5)
    keep = make_keep(flags, query_shards, shards, first, rows, text_rows)
    weights = jnp.where(keep, jnp.exp(scores), jnp.float32(0.0))
    denom = denom + jnp.sum(weights, axis=(2, 3))
    numer = numer + jnp.einsum(
        "hqsk,skhd->hqd",
        weights.astype(jnp.bfloat16),
        values_four,
        preferred_element_type=jnp.float32,
    )
    return (numer, denom)


def body(q_img, k_img, v_img, q_txt, k_txt, v_txt, norm_gains, block_map):
    rows, width = q_img.shape
    head_size = norm_gains.shape[1]
    heads = width // head_size
    text_rows = q_txt.shape[0]
    stride = rows + text_rows
    queries = jnp.concatenate(
        [normed(q_img, norm_gains[0], heads), normed(q_txt, norm_gains[2], heads)], axis=0
    )
    keys_image = normed(k_img, norm_gains[1], heads).reshape(rows, width)
    keys_text = normed(k_txt, norm_gains[3], heads).reshape(text_rows, width)
    local_keys = jnp.concatenate([keys_image, keys_text], axis=0)
    local_values = jnp.concatenate([v_img, v_txt], axis=0)
    start_state = (
        jnp.zeros((heads, stride, head_size), jnp.float32),
        jnp.zeros((heads, stride), jnp.float32),
    )

    def fold_step(carry, pieces, start):
        return accumulate(queries, block_map, 1, rows, text_rows, carry, pieces, start)

    whole_keys, whole_values = (
        lax.all_gather(local_keys, "seq", axis=0, tiled=True),
        lax.all_gather(local_values, "seq", axis=0, tiled=True),
    )
    count_seq = lax.axis_size("seq")
    grouped = 1
    while (
        grouped * 2 <= count_seq
        and count_seq % (grouped * 2) == 0
        and (grouped * 2 * stride <= 1024)
    ):
        grouped = grouped * 2
    span = grouped * stride

    def step_over(index, carry):
        offset = index * span
        piece_keys = lax.dynamic_slice_in_dim(whole_keys, offset, span, 0)
        piece_values = lax.dynamic_slice_in_dim(whole_values, offset, span, 0)
        return fold_step(carry, (piece_keys, piece_values), offset)

    numer, denom = lax.fori_loop(0, count_seq // grouped, step_over, start_state)
    result = numer / denom[..., None]
    merged = result.transpose(1, 0, 2).reshape(stride, width).astype(jnp.bfloat16)
    image_part = merged[:rows]
    text_out = merged[rows:]
    sections = lax.axis_size("section")
    image_out = lax.all_to_all(
        image_part.reshape(rows // sections, sections, width),
        "section",
        split_axis=1,
        concat_axis=2,
        tiled=True,
    )
    return (image_out, text_out)


def solution(mesh):
    placed = (
        P("seq", "section"),
        P("seq", "section"),
        P("seq", "section"),
        P("seq", "section"),
        P("seq", "section"),
        P("seq", "section"),
        P(),
        P("section", "seq", None),
    )
    return jax.shard_map(
        body,
        mesh=mesh,
        in_specs=placed,
        out_specs=(P("seq", "section", None), P("seq", "section")),
        check_vma=False,
    )
```

profile of v0, /device:TPU:0, one launch (start us, length us, event | category | flops | bytes accessed | tf_op | source)
XLA Modules:
  0.0 156.3 jit_solution(658647169518875037)
XLA Ops:
  7.3 0.9 slice_bitcast_fusion.2
  8.1 1.1 copy.71
  9.3 0.8 convert_multiply_fusion.5
  10.5 0.8 fusion.27
  11.8 0.8 copy.75
  14.8 48.2 %all-gather.3.cloned.1.call-done = bf16[1280,768]{1,0:T(8,128)(2,1)} async-done(((bf16[160,768]{1,0:T(8,128)(2,1)}), bf16[1280,768]{1,0:T(8,128)(2,1)}) %all-gather.3.cloned.1.call-update) | async-done | bytes 1966096 | tf_op jit(solution)/shard_map/all_gather | solution.py:80
  63.0 48.8 %all-gather.5.cloned.1.call-done = bf16[1280,768]{1,0:T(8,128)(2,1)} async-done(((bf16[160,768]{1,0:T(8,128)(2,1)}), bf16[1280,768]{1,0:T(8,128)(2,1)}) %all-gather.5.cloned.1.call-update) | async-done | bytes 1966096 | tf_op jit(solution)/shard_map/all_gather | solution.py:81
  111.8 25.8 %while.18 = (s32[]{:T(128)}, f32[6,160,128]{2,1,0:T(8,128)}, f32[6,160]{1,0:T(8,128)S(1)}, s32[6,1,8]{0,2,1:T(8,128)S(1)}, bf16[1280,768]{1,0:T(8,128)(2,1)}, /*...) while((s32[]{:T(128)}, f32[6,160,128]{2,1,0:T(8,128)}, ...), condition=%wide.region_6.7_spmd.clone, body=%wide.region_4.6_spmd.clone.sunk | while | flops 318505952 | bytes 18742800 | solution.py:99
  112.0 1.0 reshape.151
  113.0 1.6 %constant_dynamic-slice_fusion.3 = (bf16[640,768]{1,0:T(8,128)(2,1)S(1)}, bf16[640,768]{1,0:T(8,128)(2,1)S(1)}) fusion(bf16[1280,768]{1,0:T(8,128)(2,1)} %get-tuple-element.350, s32[]{:T(128)S(6)} %select_n.67, bf16[1280,768]{1,0:T(8,128)(2,1)} %get-tuple-element.348), kind=kLoop, calls=%fused_computation.15.clone.1 | loop fusion | bytes 3932164 | tf_op jit(solution)/shard_map/while/body/eval_jaxpr/dynamic_slice | solution.py:96
  114.6 1.2 reshape.152
  115.8 3.9 %fusion.38 = (f32[6,160]{1,0:T(8,128)S(1)}, f32[6,4,160,160]{3,2,1,0:T(8,128)}) fusion(pred[6,1,128,4,128]{2,4,3,0,1:T(32,128)(4,1)} %reshape.151, bf16[160,6,128]{2,0,1:T(8,128)(2,1)S(1)} %get-tuple-element.349, bf16[4,160,6,128]{3,2,1,0:T(8,128)(2,1)S(1)} %reshape.152), kind=kOutput, calls=%fused_computation.1.clone.1 | convolution fusion | flops 159128640 | bytes 4083456 | tf_op jit(solution)/shard_map/while/body/eval_jaxpr/qhd,skhd->hqsk/dot_general | solution.py:43
  119.6 1.1 reshape.153
  120.8 3.9 %fusion.39 = f32[6,160,128]{2,1,0:T(8,128)} fusion(f32[6,4,160,160]{3,2,1,0:T(8,128)} %get-tuple-element.313, pred[6,1,128,4,128]{2,4,3,0,1:T(32,128)(4,1)S(1)} %copy-done, bf16[4,160,6,128]{3,2,1,0:T(8,128)(2,1)S(1)} %reshape.153, f32[6,160,128]{2,1,0:T(8,128)} %get-tuple-element.331, pred[]{:T(512)S(6)} %compare.4), kind=kOutput, calls=%fused_computation.7.clone.1 | convolution fusion | flops 159375360 | bytes 4816897 | tf_op jit(solution)/shard_map/while/body/eval_jaxpr/hqsk,skhd->hqd/dot_general | solution.py:49
  124.8 1.0 reshape.151
  125.8 1.6 %constant_dynamic-slice_fusion.3 = (bf16[640,768]{1,0:T(8,128)(2,1)S(1)}, bf16[640,768]{1,0:T(8,128)(2,1)S(1)}) fusion(bf16[1280,768]{1,0:T(8,128)(2,1)} %get-tuple-element.350, s32[]{:T(128)S(6)} %select_n.67, bf16[1280,768]{1,0:T(8,128)(2,1)} %get-tuple-element.348), kind=kLoop, calls=%fused_computation.15.clone.1 | loop fusion | bytes 3932164 | tf_op jit(solution)/shard_map/while/body/eval_jaxpr/dynamic_slice | solution.py:96
  127.4 1.2 reshape.152
  128.6 3.9 %fusion.38 = (f32[6,160]{1,0:T(8,128)S(1)}, f32[6,4,160,160]{3,2,1,0:T(8,128)}) fusion(pred[6,1,128,4,128]{2,4,3,0,1:T(32,128)(4,1)} %reshape.151, bf16[160,6,128]{2,0,1:T(8,128)(2,1)S(1)} %get-tuple-element.349, bf16[4,160,6,128]{3,2,1,0:T(8,128)(2,1)S(1)} %reshape.152), kind=kOutput, calls=%fused_computation.1.clone.1 | convolution fusion | flops 159128640 | bytes 4083456 | tf_op jit(solution)/shard_map/while/body/eval_jaxpr/qhd,skhd->hqsk/dot_general | solution.py:43
  132.5 1.1 reshape.153
  133.6 4.0 %fusion.39 = f32[6,160,128]{2,1,0:T(8,128)} fusion(f32[6,4,160,160]{3,2,1,0:T(8,128)} %get-tuple-element.313, pred[6,1,128,4,128]{2,4,3,0,1:T(32,128)(4,1)S(1)} %copy-done, bf16[4,160,6,128]{3,2,1,0:T(8,128)(2,1)S(1)} %reshape.153, f32[6,160,128]{2,1,0:T(8,128)} %get-tuple-element.331, pred[]{:T(512)S(6)} %compare.4), kind=kOutput, calls=%fused_computation.7.clone.1 | convolution fusion | flops 159375360 | bytes 4816897 | tf_op jit(solution)/shard_map/while/body/eval_jaxpr/hqsk,skhd->hqd/dot_general | solution.py:49
  137.6 1.2 fusion.25
  139.8 3.4 %all-to-all-start = ((bf16[32,4,768]{2,0,1:T(8,128)(2,1)}), bf16[32,4,768]{2,0,1:T(8,128)(2,1)S(1)}, u32[]{:S(2)}, u32[]{:S(2)}) async-start(bf16[32,4,768]{2,0,1:T(8,128)(2,1)} %copy.83), calls=%async_computation | async-start | bytes 393216 | tf_op jit(solution)/shard_map/all_to_all | solution.py:105
  143.8 4.7 %all-to-all-done = bf16[32,4,768]{2,0,1:T(8,128)(2,1)S(1)} async-done(((bf16[32,4,768]{2,0,1:T(8,128)(2,1)}), bf16[32,4,768]{2,0,1:T(8,128)(2,1)S(1)}, u32[]{:S(2)}, u32[]{:S(2)}) %all-to-all-start) | async-done | bytes 196640 | tf_op jit(solution)/shard_map/all_to_all | solution.py:105
  148.7 0.8 all_to_all.10
  (59 shorter events, 5.0 us)
Async XLA Ops:
  7.2 5.5 %copy-start.3 = (bf16[128,768]{1,0:T(8,128)(2,1)S(1)}, bf16[128,768]{1,0:T(8,128)(2,1)}, u32[]{:S(2)}) copy-start(bf16[128,768]{1,0:T(8,128)(2,1)} %param.12) | copy-start | bytes 589828
  7.2 5.5 %copy-start.4 = (bf16[32,768]{1,0:T(8,128)(2,1)S(1)}, bf16[32,768]{1,0:T(8,128)(2,1)}, u32[]{:S(2)}) copy-start(bf16[32,768]{1,0:T(8,128)(2,1)} %param.15) | copy-start | bytes 147460
  7.2 6.3 %copy-start.1 = (bf16[128,768]{1,0:T(8,128)(2,1)S(1)}, bf16[128,768]{1,0:T(8,128)(2,1)}, u32[]{:S(2)}) copy-start(bf16[128,768]{1,0:T(8,128)(2,1)} %param.10) | copy-start | bytes 589828
  7.2 6.5 %copy-start.2 = (bf16[32,768]{1,0:T(8,128)(2,1)S(1)}, bf16[32,768]{1,0:T(8,128)(2,1)}, u32[]{:S(2)}) copy-start(bf16[32,768]{1,0:T(8,128)(2,1)} %param.13) | copy-start | bytes 147460
  7.2 55.8 %all-gather.3.cloned.1.call-start = ((), (), s32[]{:S(2)}) async-start(), calls=%async_computation.1 | async-start | bytes 2211840 | tf_op jit(solution)/shard_map/all_gather | solution.py:80
  9.2 5.5 %copy-start.5 = (s32[6,1,8]{2,1,0:T(1,128)S(1)}, s32[6,1,8]{2,1,0:T(1,128)}, u32[]{:S(2)}) copy-start(s32[6,1,8]{2,1,0:T(1,128)} %param.17) | copy-start | bytes 580
  12.7 99.2 %all-gather.5.cloned.1.call-start = ((), (), s32[]{:S(2)}) async-start(), calls=%async_computation.2 | async-start | bytes 2211840 | tf_op jit(solution)/shard_map/all_gather | solution.py:81
  115.7 5.0 %copy-start = (pred[6,1,128,4,128]{2,4,3,0,1:T(32,128)(4,1)S(1)}, pred[6,1,128,4,128]{2,4,3,0,1:T(32,128)(4,1)}, u32[]{:S(2)}) copy-start(pred[6,1,128,4,128]{2,4,3,0,1:T(32,128)(4,1)} %reshape.151) | copy-start | bytes 1179652 | tf_op jit(solution)/shard_map/while
  128.6 5.0 %copy-start = (pred[6,1,128,4,128]{2,4,3,0,1:T(32,128)(4,1)S(1)}, pred[6,1,128,4,128]{2,4,3,0,1:T(32,128)(4,1)}, u32[]{:S(2)}) copy-start(pred[6,1,128,4,128]{2,4,3,0,1:T(32,128)(4,1)} %reshape.151) | copy-start | bytes 1179652 | tf_op jit(solution)/shard_map/while
  139.8 8.7 %all-to-all-start = ((bf16[32,4,768]{2,0,1:T(8,128)(2,1)}), bf16[32,4,768]{2,0,1:T(8,128)(2,1)S(1)}, u32[]{:S(2)}, u32[]{:S(2)}) async-start(bf16[32,4,768]{2,0,1:T(8,128)(2,1)} %copy.83), calls=%async_computation | async-start | bytes 393216 | tf_op jit(solution)/shard_map/all_to_all | solution.py:105
Sparse Core Ops, SparseCore 0:
  12.8 50.2 all-gather.2
  65.2 46.5 all-gather.4
where the time goes:
time: 157 us; the launch traced here: 156 us
  waiting for transfers between devices  102 us (65%)
  local copies, waits for them, and re-layouts  16.6 us (11%)
  matrix products  15.6 us (10%)
  between operations  14.3 us (9%)
  other arithmetic  4.48 us (3%)
  starting transfers between devices  3.45 us (2%)
    all_gather x1, waiting for transfers between devices, body(): lax.all_gather(local_values, 'seq', axis=0, tiled=True)  48.8 us
    all_gather x1, waiting for transfers between devices, body(): lax.all_gather(local_keys, 'seq', axis=0, tiled=True)  48.2 us
    dot_general x2, matrix products, accumulate(): jnp.einsum('hqsk,skhd->hqd', weights.astype(jnp.bfloat16), values_four, p...  7.92 us
    dot_general x2, matrix products, accumulate(): jnp.einsum('qhd,skhd->hqsk', queries, keys_four, preferred_element_type=j...  7.7 us
    all_to_all x1, waiting for transfers between devices, body(): lax.all_to_all(image_part.reshape(rows // sections, sections, width), 'se...  4.68 us
    all_to_all x1, starting transfers between devices, body(): lax.all_to_all(image_part.reshape(rows // sections, sections, width), 'se...  3.37 us
    dynamic_slice x2, local copies, waits for them, and re-layouts, step_over(): piece_values = lax.dynamic_slice_in_dim(whole_values, offset, span, 0)  3.25 us
  transfers between devices with their start and end apart: 3, of which 3 were waited for; matrix products, arithmetic and copies ran while one was open for 2% of the time, Pallas kernels for 0%

commit v1 on v0

--- a/solution.py
+++ b/solution.py
@@ -1,6 +1,11 @@
+import functools
+import math
+
 import jax
 import jax.numpy as jnp
 from jax import lax
+from jax.experimental import pallas as pl
+from jax.experimental.pallas import tpu as pltpu
 from jax.sharding import PartitionSpec as P
 
 BLOCK = 128
@@ -112,6 +117,380 @@
     return (image_out, text_out)
 
 
+def owner_of(head, heads, odd):
+    even_pick = head + lax.div(head + heads - 2, heads - 1) + lax.div(head, heads - 1)
+    return odd * (head + 1) + (1 - odd) * even_pick
+
+
+def head_of(place, heads, odd):
+    last = heads + 1
+    even_pick = place - lax.div(place + last - 1, last) - lax.div(place, last)
+    return odd * (place - 1) + (1 - odd) * even_pick
+
+
+def partner(place, step, count):
+    total = 0
+    bit = 1
+    while bit < count:
+        total = total + bit * lax.rem(lax.div(place, bit) + lax.div(step, bit), 2)
+        bit *= 2
+    return total
+
+
+def head_kernel(
+    heads, seqs, sections,
+    q_img, k_img, v_img, q_txt, k_txt, v_txt, gains, flags_in,
+    image_out, text_out,
+    flags_own, flags_got, q_img_got, q_txt_got, k_img_got, k_txt_got, values, keys_t, total,
+    image_stage, text_stage,
+    send_sem, recv_sem, image_sent, text_sent, image_recv, text_recv,
+):
+    rows = q_img.shape[0]
+    text_rows = q_txt.shape[0]
+    size = gains.shape[1]
+    key_blocks = flags_in.shape[2]
+    part = rows // sections
+    all_rows = seqs * rows
+    factor = size ** (-0.5) * math.log2(math.e)
+    section = lax.axis_index("section")
+    me = lax.axis_index("seq")
+    odd = lax.rem(section, 2)
+
+    barrier = pltpu.get_barrier_semaphore()
+
+    def greet(index, carry):
+        to_section = lax.div(index, seqs)
+        to_seq = lax.rem(index, seqs)
+
+        @pl.when(jnp.logical_or(to_section != section, to_seq != me))
+        def _():
+            pl.semaphore_signal(
+                barrier,
+                inc=1,
+                device_id={"section": to_section, "seq": to_seq},
+                device_id_type=pl.DeviceIdType.MESH,
+            )
+
+        return carry
+
+    lax.fori_loop(0, sections * seqs, greet, 0)
+    for head in range(heads):
+        for block in range(key_blocks):
+            flags_own[head, block : block + 1, :] = jnp.full(
+                (1, flags_own.shape[2]), flags_in[head, 0, block], jnp.int32
+            )
+    pl.semaphore_wait(barrier, sections * seqs - 1)
+
+    def landing(kind, source):
+        if kind == 0:
+            return flags_got.at[source]
+        if kind == 1:
+            return k_img_got.at[source]
+        if kind == 2:
+            return k_txt_got.at[source]
+        if kind == 3:
+            return values.at[pl.ds(pl.multiple_of(source * rows, rows), rows)]
+        if kind == 4:
+            return values.at[pl.ds(pl.multiple_of(all_rows + source * text_rows, text_rows), text_rows)]
+        if kind == 5:
+            return q_img_got.at[source]
+        return q_txt_got.at[source]
+
+    operands = (None, k_img, k_txt, v_img, v_txt, q_img, q_txt)
+
+    def leaving(kind, head):
+        if kind == 0:
+            return flags_own.at[head]
+        return operands[kind].at[:, pl.ds(pl.multiple_of(head * size, size), size)]
+
+    def outward(kind, head):
+        return pltpu.make_async_remote_copy(
+            src_ref=leaving(kind, head),
+            dst_ref=landing(kind, me),
+            send_sem=send_sem.at[kind, head],
+            recv_sem=recv_sem.at[kind, me],
+            device_id={"seq": owner_of(head, heads, odd)},
+            device_id_type=pl.DeviceIdType.MESH,
+        )
+
+    def inward(kind, source):
+        place = landing(kind, source)
+        return pltpu.make_async_copy(place, place, recv_sem.at[kind, source])
+
+    for group in ((0, 1, 2), (3, 4), (5, 6)):
+
+        def send_group(step, carry):
+            head = lax.rem(step + me, heads)
+            target = owner_of(head, heads, odd)
+
+            @pl.when(target != me)
+            def _():
+                for kind in group:
+                    outward(kind, head).start()
+
+            @pl.when(target == me)
+            def _():
+                for kind in group:
+                    pltpu.make_async_copy(
+                        leaving(kind, head), landing(kind, me), recv_sem.at[kind, me]
+                    ).start()
+
+            return carry
+
+        lax.fori_loop(0, heads, send_group, 0)
+
+    def scaled(block, gain_row):
+        floats = block.astype(jnp.float32)
+        power = jnp.mean(floats * floats, axis=-1, keepdims=True)
+        return floats * lax.rsqrt(power + 1e-06) * gains[gain_row : gain_row + 1, :]
+
+    my_head = head_of(me, heads, odd)
+    mine = jnp.logical_and(my_head >= 0, my_head < heads)
+    mine = jnp.logical_and(mine, owner_of(my_head, heads, odd) == me)
+
+    def image_copy(chunk, to_section):
+        column = pl.multiple_of((section * heads + my_head) * size, size)
+        return (
+            image_stage.at[chunk, to_section],
+            image_out.at[:, pl.ds(column, size)],
+        )
+
+    def image_remote(chunk, to_section):
+        source, target = image_copy(chunk, to_section)
+        return pltpu.make_async_remote_copy(
+            src_ref=source,
+            dst_ref=target,
+            send_sem=image_sent.at[chunk, to_section],
+            recv_sem=image_recv.at[section * heads + my_head],
+            device_id={"section": to_section, "seq": chunk},
+            device_id_type=pl.DeviceIdType.MESH,
+        )
+
+    def text_copy(chunk):
+        return (
+            text_stage.at[chunk],
+            text_out.at[:, pl.ds(pl.multiple_of(my_head * size, size), size)],
+        )
+
+    def text_remote(chunk):
+        source, target = text_copy(chunk)
+        return pltpu.make_async_remote_copy(
+            src_ref=source,
+            dst_ref=target,
+            send_sem=text_sent.at[chunk],
+            recv_sem=text_recv.at[my_head],
+            device_id={"seq": chunk},
+            device_id_type=pl.DeviceIdType.MESH,
+        )
+
+    @pl.when(mine)
+    def _():
+        def take_keys(step, carry):
+            source = partner(me, step, seqs)
+            inward(0, source).wait()
+            inward(1, source).wait()
+            inward(2, source).wait()
+            keys_t[:, pl.ds(pl.multiple_of(source * rows, rows), rows)] = (
+                scaled(k_img_got[source], 1).T.astype(jnp.bfloat16)
+            )
+            return carry
+
+        lax.fori_loop(0, seqs, take_keys, 0)
+        text_keys = k_txt_got[...].reshape(seqs * text_rows, size)
+        keys_t[:, all_rows:] = scaled(text_keys, 3).T.astype(jnp.bfloat16)
+
+        def take_values(step, carry):
+            source = partner(me, step, seqs)
+            inward(3, source).wait()
+            inward(4, source).wait()
+            return carry
+
+        lax.fori_loop(0, seqs, take_values, 0)
+
+        def answer(step, carry):
+            chunk = partner(me, step, seqs)
+            inward(5, chunk).wait()
+            inward(6, chunk).wait()
+            queries = jnp.concatenate(
+                [scaled(q_img_got[chunk], 0), scaled(q_txt_got[chunk], 2)], axis=0
+            ).astype(jnp.bfloat16)
+            flags = flags_got[chunk]
+            numer = jnp.zeros((rows + text_rows, size), jnp.float32)
+            denom = jnp.zeros((rows + text_rows, rows), jnp.float32)
+            width = 2 * rows
+            for first in range(0, keys_t.shape[1], width):
+                scores = jnp.dot(
+                    queries, keys_t[:, first : first + width], preferred_element_type=jnp.float32
+                )
+                weights = jnp.exp2(scores * factor)
+                halves = []
+                for half in range(2):
+                    piece = weights[:, half * rows : (half + 1) * rows]
+                    block = first // rows + half
+                    if first < all_rows:
+                        kept = jnp.where(flags[block : block + 1, :] > 0, piece[:rows], 0.0)
+                        piece = jnp.concatenate([kept, piece[rows:]], axis=0)
+                    denom = denom + piece
+                    halves.append(piece.astype(jnp.bfloat16))
+                numer = numer + jnp.dot(
+                    jnp.concatenate(halves, axis=1),
+                    values[first : first + width, :],
+                    preferred_element_type=jnp.float32,
+                )
+            total[...] = numer / jnp.sum(denom, axis=-1, keepdims=True)
+            for to_section in range(sections):
+                image_stage[chunk, to_section] = total[
+                    pl.ds(to_section, part, stride=sections), :
+                ].astype(jnp.bfloat16)
+            text_stage[chunk] = total[rows:, :].astype(jnp.bfloat16)
+            for to_section in range(sections):
+                here = jnp.logical_and(section == to_section, chunk == me)
+
+                @pl.when(jnp.logical_not(here))
+                def _():
+                    image_remote(chunk, to_section).start()
+
+                @pl.when(here)
+                def _():
+                    source, target = image_copy(chunk, to_section)
+                    pltpu.make_async_copy(
+                        source, target, image_recv.at[section * heads + my_head]
+                    ).start()
+
+            @pl.when(chunk != me)
+            def _():
+                text_remote(chunk).start()
+
+            @pl.when(chunk == me)
+            def _():
+                source, target = text_copy(chunk)
+                pltpu.make_async_copy(source, target, text_recv.at[my_head]).start()
+
+            return carry
+
+        lax.fori_loop(0, seqs, answer, 0)
+
+    def finish_group(step, carry):
+        head = lax.rem(step + me, heads)
+
+        @pl.when(owner_of(head, heads, odd) != me)
+        def _():
+            for kind in range(7):
+                outward(kind, head).wait_send()
+
+        return carry
+
+    lax.fori_loop(0, heads, finish_group, 0)
+
+    @pl.when(mine)
+    def _():
+        def sent(chunk, carry):
+            for to_section in range(sections):
+
+                @pl.when(jnp.logical_or(section != to_section, chunk != me))
+                def _():
+                    image_remote(chunk, to_section).wait_send()
+
+            @pl.when(chunk != me)
+            def _():
+                text_remote(chunk).wait_send()
+
+            return carry
+
+        lax.fori_loop(0, seqs, sent, 0)
+
+    def arrived(head, carry):
+        place = image_out.at[:, pl.ds(pl.multiple_of(head * size, size), size)]
+        pltpu.make_async_copy(place, place, image_recv.at[head]).wait()
+        return carry
+
+    lax.fori_loop(0, sections * heads, arrived, 0)
+
+    def text_arrived(head, carry):
+        place = text_out.at[:, pl.ds(pl.multiple_of(head * size, size), size)]
+        pltpu.make_async_copy(place, place, text_recv.at[head]).wait()
+        return carry
+
+    lax.fori_loop(0, heads, text_arrived, 0)
+
+
+def by_heads(q_img, k_img, v_img, q_txt, k_txt, v_txt, norm_gains, block_map):
+    rows, width = q_img.shape
+    size = norm_gains.shape[1]
+    heads = width // size
+    text_rows = q_txt.shape[0]
+    seqs = lax.axis_size("seq")
+    sections = lax.axis_size("section")
+    half = jnp.bfloat16
+    flags_shape = (block_map.shape[2], size)
+    anywhere = pl.BlockSpec(memory_space=pl.ANY)
+    dma = pltpu.SemaphoreType.DMA
+    image_flat, text_out = pl.pallas_call(
+        functools.partial(head_kernel, heads, seqs, sections),
+        out_shape=(
+            jax.ShapeDtypeStruct((rows // sections, sections * width), half),
+            jax.ShapeDtypeStruct((text_rows, width), half),
+        ),
+        in_specs=[anywhere] * 6
+        + [pl.BlockSpec(memory_space=pltpu.VMEM), pl.BlockSpec(memory_space=pltpu.SMEM)],
+        out_specs=(anywhere, anywhere),
+        scratch_shapes=[
+            pltpu.VMEM((heads,) + flags_shape, jnp.int32),
+            pltpu.VMEM((seqs,) + flags_shape, jnp.int32),
+            pltpu.VMEM((seqs, rows, size), half),
+            pltpu.VMEM((seqs, text_rows, size), half),
+            pltpu.VMEM((seqs, rows, size), half),
+            pltpu.VMEM((seqs, text_rows, size), half),
+            pltpu.VMEM((seqs * (rows + text_rows), size), half),
+            pltpu.VMEM((size, seqs * (rows + text_rows)), half),
+            pltpu.VMEM((rows + text_rows, size), jnp.float32),
+            pltpu.VMEM((seqs, sections, rows // sections, size), half),
+            pltpu.VMEM((seqs, text_rows, size), half),
+            dma((7, heads)),
+            dma((7, seqs)),
+            dma((seqs, sections)),
+            dma((seqs,)),
+            dma((sections * heads,)),
+            dma((heads,)),
+        ],
+        compiler_params=pltpu.CompilerParams(
+            collective_id=0, has_side_effects=True, vmem_limit_bytes=32 * 1024 * 1024
+        ),
+    )(q_img, k_img, v_img, q_txt, k_txt, v_txt, norm_gains, block_map)
+    return (image_flat.reshape(rows // sections, 1, sections * width), text_out)
+
+
+def one_head_fits(rows, text_rows, heads, head_size, key_blocks, seqs, sections):
+    return (
+        rows == BLOCK
+        and head_size == BLOCK
+        and seqs == heads + 2
+        and seqs & (seqs - 1) == 0
+        and key_blocks == seqs
+        and seqs % 8 == 0
+        and text_rows % 16 == 0
+        and (seqs * text_rows) % (2 * BLOCK) == 0
+        and rows % (16 * sections) == 0
+        and sections % 2 == 0
+    )
+
+
+def layer(q_img, k_img, v_img, q_txt, k_txt, v_txt, norm_gains, block_map):
+    rows, width = q_img.shape
+    head_size = norm_gains.shape[1]
+    fits = one_head_fits(
+        rows,
+        q_txt.shape[0],
+        width // head_size,
+        head_size,
+        block_map.shape[2],
+        lax.axis_size("seq"),
+        lax.axis_size("section"),
+    )
+    chosen = by_heads if fits else body
+    return chosen(q_img, k_img, v_img, q_txt, k_txt, v_txt, norm_gains, block_map)
+
+
 def solution(mesh):
     placed = (
         P("seq", "section"),
@@ -124,7 +503,7 @@
         P("section", "seq", None),
     )
     return jax.shard_map(
-        body,
+        layer,
         mesh=mesh,
         in_specs=placed,
         out_specs=(P("seq", "section", None), P("seq", "section")),

time: 157 us -> 43.5 us (0.28)
  waiting for transfers between devices: 102 us -> 0 us
  Pallas kernels: 0 us -> 34.6 us
  matrix products: 15.6 us -> 0 us
  between operations: 14.3 us -> 0.66 us
  local copies, waits for them, and re-layouts: 16.6 us -> 7.83 us
  other arithmetic: 4.48 us -> 0 us
  starting transfers between devices: 3.45 us -> 0 us
    all_gather x2 -> x0, waiting for transfers between devices: 97.1 us -> none  [the longest x1 48.8 us: body(): lax.all_gather(local_values, 'seq', axis=0, tiled=True)]
    pallas_call x0 -> x1, Pallas kernels: none -> 34.6 us  [by_heads(): pl.pallas_call(functools.partial(head_kernel, heads, seqs, sections), out...]
    dot_general x4 -> x0, matrix products: 15.6 us -> none  [the longest x2 7.92 us: accumulate(): jnp.einsum('hqsk,skhd->hqd', weights.astype(jnp.bfloat16), values_four, p...]
    reshape x9 -> x0, local copies, waits for them, and re-layouts: 7.46 us -> none  [the longest x2 2.32 us: accumulate(): keys_four = piece_keys.reshape(shards, stride, heads, head_size)]
    unnamed x14 -> x18, local copies, waits for them, and re-layouts: 1.56 us -> 7.83 us
    all_to_all x1 -> x0, waiting for transfers between devices: 4.68 us -> none  [body(): lax.all_to_all(image_part.reshape(rows // sections, sections, width), 'se...]
    all_to_all x1 -> x0, starting transfers between devices: 3.37 us -> none  [body(): lax.all_to_all(image_part.reshape(rows // sections, sections, width), 'se...]
    dynamic_slice x2 -> x0, local copies, waits for them, and re-layouts: 3.25 us -> none  [step_over(): piece_values = lax.dynamic_slice_in_dim(whole_values, offset, span, 0)]
  transfers between devices with their start and end apart: 3 -> 0, of which waited for: 3 -> 0; matrix products, arithmetic and copies ran while one was open for 2% -> 0% of each run, Pallas kernels for 0% -> 0%
where the time goes in v1:
time: 43.5 us; the launch traced here: 43.1 us
  Pallas kernels  34.6 us (80%)
  local copies, waits for them, and re-layouts  7.83 us (18%)
  between operations  0.66 us (2%)
    pallas_call x1, Pallas kernels, by_heads(): pl.pallas_call(functools.partial(head_kernel, heads, seqs, sections), out...  34.6 us
    unnamed x18, local copies, waits for them, and re-layouts  7.83 us

profile of v1, /device:TPU:0, one launch (start us, length us, event | category | flops | bytes accessed | tf_op | source)
XLA Modules:
  0.0 43.1 jit_solution(2922384943445913331)
XLA Ops:
  0.6 0.0 copy-start
  0.6 0.9 %copy-done = bf16[128,768]{1,0:T(8,128)(2,1)S(1)} copy-done((bf16[128,768]{1,0:T(8,128)(2,1)S(1)}, bf16[128,768]{1,0:T(8,128)(2,1)}, u32[]{:S(2)}) %copy-start) | copy-done | bytes 196632
  1.6 0.0 copy-start.1
  1.6 0.9 %copy-done.1 = bf16[128,768]{1,0:T(8,128)(2,1)S(1)} copy-done((bf16[128,768]{1,0:T(8,128)(2,1)S(1)}, bf16[128,768]{1,0:T(8,128)(2,1)}, u32[]{:S(2)}) %copy-start.1) | copy-done | bytes 196632
  2.5 0.0 copy-start.2
  2.5 0.9 %copy-done.2 = bf16[128,768]{1,0:T(8,128)(2,1)S(1)} copy-done((bf16[128,768]{1,0:T(8,128)(2,1)S(1)}, bf16[128,768]{1,0:T(8,128)(2,1)}, u32[]{:S(2)}) %copy-start.2) | copy-done | bytes 196632
  3.4 0.0 copy-start.3
  3.4 0.8 %copy-done.3 = bf16[32,768]{1,0:T(8,128)(2,1)S(1)} copy-done((bf16[32,768]{1,0:T(8,128)(2,1)S(1)}, bf16[32,768]{1,0:T(8,128)(2,1)}, u32[]{:S(2)}) %copy-start.3) | copy-done | bytes 49176
  4.2 0.0 copy-start.4
  4.2 0.8 %copy-done.4 = bf16[32,768]{1,0:T(8,128)(2,1)S(1)} copy-done((bf16[32,768]{1,0:T(8,128)(2,1)S(1)}, bf16[32,768]{1,0:T(8,128)(2,1)}, u32[]{:S(2)}) %copy-start.4) | copy-done | bytes 49176
  5.0 0.0 copy-start.5
  5.0 0.8 %copy-done.5 = bf16[32,768]{1,0:T(8,128)(2,1)S(1)} copy-done((bf16[32,768]{1,0:T(8,128)(2,1)S(1)}, bf16[32,768]{1,0:T(8,128)(2,1)}, u32[]{:S(2)}) %copy-start.5) | copy-done | bytes 49176
  5.8 0.0 copy-start.6
  5.8 0.7 %copy-done.6 = s32[6,1,8]{2,1,0:T(1,128)S(1)} copy-done((s32[6,1,8]{2,1,0:T(1,128)S(1)}, s32[6,1,8]{2,1,0:T(1,128)}, u32[]{:S(2)}) %copy-start.6) | copy-done | bytes 216
  6.5 0.0 copy-start.7
  6.5 0.7 %copy-done.7 = f32[4,128]{1,0:T(4,128)S(1)} copy-done((f32[4,128]{1,0:T(4,128)S(1)}, f32[4,128]{1,0:T(4,128)}, u32[]{:S(2)}) %copy-start.7) | copy-done | bytes 2072
  7.2 34.6 %shard_map.95 = (bf16[32,3072]{1,0:T(8,128)(2,1)S(1)}, bf16[32,768]{1,0:T(8,128)(2,1)S(1)}) custom-call(bf16[128,768]{1,0:T(8,128)(2,1)S(1)} %copy-done, bf16[128,768]{1,0:T(8,128)(2,1)S(1)} %copy-done.1, bf16[128,768]{1,0:T(8,128)(2,1)S(1)} %copy-done.2, bf16[32,768]{1,0:T(8,128)(2,1)S(1)} %copy-done.3, bf16[32,768]{1,0:T(8,128)(2,1)S(1)} %copy-done.4, ...), custom_call_target="tpu_custom_call" | custom-call | tf_op jit(solution)/shard_map/pallas_call | solution.py:428
  41.8 0.7 %copy.12 = bf16[32,1,3072]{2,0,1:T(8,128)(2,1)} copy(bf16[32,1,3072]{2,0,1:T(8,128)(2,1)S(1)} %bitcast.1) | data formatting | bytes 393216
  42.4 0.6 %copy.13 = bf16[32,768]{1,0:T(8,128)(2,1)} copy(bf16[32,768]{1,0:T(8,128)(2,1)S(1)} %get-tuple-element.9) | data formatting | bytes 98304
Async XLA Ops:
  0.6 0.9 %copy-start = (bf16[128,768]{1,0:T(8,128)(2,1)S(1)}, bf16[128,768]{1,0:T(8,128)(2,1)}, u32[]{:S(2)}) copy-start(bf16[128,768]{1,0:T(8,128)(2,1)} %q_img.1) | copy-start | bytes 589828
  1.6 0.9 %copy-start.1 = (bf16[128,768]{1,0:T(8,128)(2,1)S(1)}, bf16[128,768]{1,0:T(8,128)(2,1)}, u32[]{:S(2)}) copy-start(bf16[128,768]{1,0:T(8,128)(2,1)} %k_img.1) | copy-start | bytes 589828
  2.5 0.9 %copy-start.2 = (bf16[128,768]{1,0:T(8,128)(2,1)S(1)}, bf16[128,768]{1,0:T(8,128)(2,1)}, u32[]{:S(2)}) copy-start(bf16[128,768]{1,0:T(8,128)(2,1)} %v_img.1) | copy-start | bytes 589828
  3.4 0.8 %copy-start.3 = (bf16[32,768]{1,0:T(8,128)(2,1)S(1)}, bf16[32,768]{1,0:T(8,128)(2,1)}, u32[]{:S(2)}) copy-start(bf16[32,768]{1,0:T(8,128)(2,1)} %q_txt.1) | copy-start | bytes 147460
  4.2 0.8 %copy-start.4 = (bf16[32,768]{1,0:T(8,128)(2,1)S(1)}, bf16[32,768]{1,0:T(8,128)(2,1)}, u32[]{:S(2)}) copy-start(bf16[32,768]{1,0:T(8,128)(2,1)} %k_txt.1) | copy-start | bytes 147460
  5.0 0.8 %copy-start.5 = (bf16[32,768]{1,0:T(8,128)(2,1)S(1)}, bf16[32,768]{1,0:T(8,128)(2,1)}, u32[]{:S(2)}) copy-start(bf16[32,768]{1,0:T(8,128)(2,1)} %v_txt.1) | copy-start | bytes 147460
  5.8 0.7 %copy-start.6 = (s32[6,1,8]{2,1,0:T(1,128)S(1)}, s32[6,1,8]{2,1,0:T(1,128)}, u32[]{:S(2)}) copy-start(s32[6,1,8]{2,1,0:T(1,128)} %flags_in.1) | copy-start | bytes 580
  6.5 0.7 %copy-start.7 = (f32[4,128]{1,0:T(4,128)S(1)}, f32[4,128]{1,0:T(4,128)}, u32[]{:S(2)}) copy-start(f32[4,128]{1,0:T(4,128)} %gains.1) | copy-start | bytes 6148

commit v2 on v1

--- a/solution.py
+++ b/solution.py
@@ -454,7 +454,7 @@
             dma((heads,)),
         ],
         compiler_params=pltpu.CompilerParams(
-            collective_id=0, has_side_effects=True, vmem_limit_bytes=32 * 1024 * 1024
+            collective_id=0, has_side_effects=True, vmem_limit_bytes=60 * 1024 * 1024
         ),
     )(q_img, k_img, v_img, q_txt, k_txt, v_txt, norm_gains, block_map)
     return (image_flat.reshape(rows // sections, 1, sections * width), text_out)

time: 43.5 us -> 38.2 us (0.88)
  local copies, waits for them, and re-layouts: 7.83 us -> 2.25 us
  Pallas kernels: 34.6 us -> 35.1 us
    unnamed x18 -> x4, local copies, waits for them, and re-layouts: 7.83 us -> 2.25 us
    pallas_call x1, Pallas kernels: 34.6 us -> 35.1 us  [by_heads(): pl.pallas_call(functools.partial(head_kernel, heads, seqs, sections), out...]
where the time goes in v2:
time: 38.2 us; the launch traced here: 38 us
  Pallas kernels  35.1 us (92%)
  local copies, waits for them, and re-layouts  2.25 us (6%)
  between operations  0.65 us (2%)
    pallas_call x1, Pallas kernels, by_heads(): pl.pallas_call(functools.partial(head_kernel, heads, seqs, sections), out...  35.1 us
    unnamed x4, local copies, waits for them, and re-layouts  2.25 us

profile of v2, /device:TPU:0, one launch (start us, length us, event | category | flops | bytes accessed | tf_op | source)
XLA Modules:
  0.0 38.0 jit_solution(400394169231656933)
XLA Ops:
  0.6 35.1 %shard_map.95 = (bf16[32,3072]{1,0:T(8,128)(2,1)}, bf16[32,768]{1,0:T(8,128)(2,1)}) custom-call(bf16[128,768]{1,0:T(8,128)(2,1)} %q_img.1, bf16[128,768]{1,0:T(8,128)(2,1)} %k_img.1, bf16[128,768]{1,0:T(8,128)(2,1)} %v_img.1, bf16[32,768]{1,0:T(8,128)(2,1)} %q_txt.1, bf16[32,768]{1,0:T(8,128)(2,1)} %k_txt.1, bf16[32,768]{1,0:T(8,128)(2,1)} %v_txt.1, ...), custom_call_target="tpu_custom_call" | custom-call | tf_op jit(solution)/shard_map/pallas_call | solution.py:428
  35.7 0.0 copy-start
  35.7 1.6 %copy.12 = bf16[32,1,3072]{2,0,1:T(8,128)(2,1)} copy(bf16[32,1,3072]{2,0,1:T(8,128)(2,1)} %bitcast.1) | data formatting | bytes 393216
  37.4 0.0 copy-done
  37.4 0.6 %copy.13 = bf16[32,768]{1,0:T(8,128)(2,1)} copy(bf16[32,768]{1,0:T(8,128)(2,1)S(1)} %copy-done) | data formatting | bytes 98304
Async XLA Ops:
  35.7 1.6 %copy-start = (bf16[32,768]{1,0:T(8,128)(2,1)S(1)}, bf16[32,768]{1,0:T(8,128)(2,1)}, u32[]{:S(2)}) copy-start(bf16[32,768]{1,0:T(8,128)(2,1)} %get-tuple-element.9) | copy-start | bytes 147460

commit v3 on v2

--- a/solution.py
+++ b/solution.py
@@ -117,15 +117,8 @@
     return (image_out, text_out)
 
 
-def owner_of(head, heads, odd):
-    even_pick = head + lax.div(head + heads - 2, heads - 1) + lax.div(head, heads - 1)
-    return odd * (head + 1) + (1 - odd) * even_pick
-
-
-def head_of(place, heads, odd):
-    last = heads + 1
-    even_pick = place - lax.div(place + last - 1, last) - lax.div(place, last)
-    return odd * (place - 1) + (1 - odd) * even_pick
+def owner_of(head):
+    return head + 1
 
 
 def partner(place, step, count):
@@ -141,9 +134,10 @@
     heads, seqs, sections,
     q_img, k_img, v_img, q_txt, k_txt, v_txt, gains, flags_in,
     image_out, text_out,
-    flags_own, flags_got, q_img_got, q_txt_got, k_img_got, k_txt_got, values, keys_t, total,
+    flags_own, flags_got, q_got, k_got, v_got, values, keys_t, total,
     image_stage, text_stage,
-    send_sem, recv_sem, image_sent, text_sent, image_recv, text_recv,
+    held_q, held_k, held_v,
+    send_sem, recv_sem, image_sent, text_sent, image_recv, text_recv, ready, load_sem,
 ):
     rows = q_img.shape[0]
     text_rows = q_txt.shape[0]
@@ -154,49 +148,51 @@
     factor = size ** (-0.5) * math.log2(math.e)
     section = lax.axis_index("section")
     me = lax.axis_index("seq")
-    odd = lax.rem(section, 2)
+
+    near = heads // 2
 
     barrier = pltpu.get_barrier_semaphore()
 
-    def greet(index, carry):
-        to_section = lax.div(index, seqs)
-        to_seq = lax.rem(index, seqs)
-
-        @pl.when(jnp.logical_or(to_section != section, to_seq != me))
-        def _():
-            pl.semaphore_signal(
-                barrier,
-                inc=1,
-                device_id={"section": to_section, "seq": to_seq},
-                device_id_type=pl.DeviceIdType.MESH,
+    loads = [
+        pltpu.make_async_copy(source, target, load_sem.at[index])
+        for index, (source, target) in enumerate(
+            (
+                (k_img, held_k.at[:rows]),
+                (k_txt, held_k.at[rows:]),
+                (v_img, held_v.at[:rows]),
+                (v_txt, held_v.at[rows:]),
+                (q_img, held_q.at[:rows]),
+                (q_txt, held_q.at[rows:]),
             )
-
-        return carry
-
-    lax.fori_loop(0, sections * seqs, greet, 0)
+        )
+    ]
+
+    def signal(semaphore, **place):
+        pl.semaphore_signal(
+            semaphore, inc=1, device_id=place, device_id_type=pl.DeviceIdType.MESH
+        )
+
+    for step in range(1, seqs):
+        signal(barrier, seq=lax.rem(me + step, seqs))
+    for step in range(1, sections):
+        signal(barrier, section=lax.rem(section + step, sections))
+    for load in loads:
+        load.start()
     for head in range(heads):
         for block in range(key_blocks):
             flags_own[head, block : block + 1, :] = jnp.full(
                 (1, flags_own.shape[2]), flags_in[head, 0, block], jnp.int32
             )
-    pl.semaphore_wait(barrier, sections * seqs - 1)
+    pl.semaphore_wait(barrier, sections + seqs - 2)
+    for step in range(1, sections):
+        signal(ready, section=lax.rem(section + step, sections))
 
     def landing(kind, source):
         if kind == 0:
             return flags_got.at[source]
-        if kind == 1:
-            return k_img_got.at[source]
-        if kind == 2:
-            return k_txt_got.at[source]
-        if kind == 3:
-            return values.at[pl.ds(pl.multiple_of(source * rows, rows), rows)]
-        if kind == 4:
-            return values.at[pl.ds(pl.multiple_of(all_rows + source * text_rows, text_rows), text_rows)]
-        if kind == 5:
-            return q_img_got.at[source]
-        return q_txt_got.at[source]
-
-    operands = (None, k_img, k_txt, v_img, v_txt, q_img, q_txt)
+        return (k_got, v_got, q_got)[kind - 1].at[source]
+
+    operands = (None, held_k, held_v, held_q)
 
     def leaving(kind, head):
         if kind == 0:
@@ -209,7 +205,7 @@
             dst_ref=landing(kind, me),
             send_sem=send_sem.at[kind, head],
             recv_sem=recv_sem.at[kind, me],
-            device_id={"seq": owner_of(head, heads, odd)},
+            device_id={"seq": owner_of(head)},
             device_id_type=pl.DeviceIdType.MESH,
         )
 
@@ -217,11 +213,16 @@
         place = landing(kind, source)
         return pltpu.make_async_copy(place, place, recv_sem.at[kind, source])
 
-    for group in ((0, 1, 2), (3, 4), (5, 6)):
+    for group in ((0, 1), (2,), (3,)):
+        for kind in group:
+            if kind > 0:
+                loads[2 * kind - 2].wait()
+                loads[2 * kind - 1].wait()
 
         def send_group(step, carry):
-            head = lax.rem(step + me, heads)
-            target = owner_of(head, heads, odd)
+            turn = lax.rem(lax.div(step, near) + 1 - lax.div(me, seqs // 2), 2)
+            head = turn * near + lax.rem(step + me, near)
+            target = owner_of(head)
 
             @pl.when(target != me)
             def _():
@@ -244,9 +245,8 @@
         power = jnp.mean(floats * floats, axis=-1, keepdims=True)
         return floats * lax.rsqrt(power + 1e-06) * gains[gain_row : gain_row + 1, :]
 
-    my_head = head_of(me, heads, odd)
+    my_head = me - 1
     mine = jnp.logical_and(my_head >= 0, my_head < heads)
-    mine = jnp.logical_and(mine, owner_of(my_head, heads, odd) == me)
 
     def image_copy(chunk, to_section):
         column = pl.multiple_of((section * heads + my_head) * size, size)
@@ -283,36 +283,39 @@
             device_id_type=pl.DeviceIdType.MESH,
         )
 
+    pl.semaphore_wait(ready, sections - 1)
+
     @pl.when(mine)
     def _():
         def take_keys(step, carry):
             source = partner(me, step, seqs)
             inward(0, source).wait()
             inward(1, source).wait()
-            inward(2, source).wait()
             keys_t[:, pl.ds(pl.multiple_of(source * rows, rows), rows)] = (
-                scaled(k_img_got[source], 1).T.astype(jnp.bfloat16)
+                scaled(k_got[source, :rows], 1).T.astype(jnp.bfloat16)
             )
             return carry
 
         lax.fori_loop(0, seqs, take_keys, 0)
-        text_keys = k_txt_got[...].reshape(seqs * text_rows, size)
+        text_keys = k_got[:, rows:].reshape(seqs * text_rows, size)
         keys_t[:, all_rows:] = scaled(text_keys, 3).T.astype(jnp.bfloat16)
 
         def take_values(step, carry):
             source = partner(me, step, seqs)
-            inward(3, source).wait()
-            inward(4, source).wait()
+            inward(2, source).wait()
+            image_place = pl.ds(pl.multiple_of(source * rows, rows), rows)
+            values[image_place, :] = v_got[source, :rows]
+            text_place = pl.multiple_of(all_rows + source * text_rows, text_rows)
+            values[pl.ds(text_place, text_rows), :] = v_got[source, rows:]
             return carry
 
         lax.fori_loop(0, seqs, take_values, 0)
 
         def answer(step, carry):
             chunk = partner(me, step, seqs)
-            inward(5, chunk).wait()
-            inward(6, chunk).wait()
+            inward(3, chunk).wait()
             queries = jnp.concatenate(
-                [scaled(q_img_got[chunk], 0), scaled(q_txt_got[chunk], 2)], axis=0
+                [scaled(q_got[chunk, :rows], 0), scaled(q_got[chunk, rows:], 2)], axis=0
             ).astype(jnp.bfloat16)
             flags = flags_got[chunk]
             numer = jnp.zeros((rows + text_rows, size), jnp.float32)
@@ -373,9 +376,9 @@
     def finish_group(step, carry):
         head = lax.rem(step + me, heads)
 
-        @pl.when(owner_of(head, heads, odd) != me)
+        @pl.when(owner_of(head) != me)
         def _():
-            for kind in range(7):
+            for kind in range(4):
                 outward(kind, head).wait_send()
 
         return carry
@@ -437,21 +440,25 @@
         scratch_shapes=[
             pltpu.VMEM((heads,) + flags_shape, jnp.int32),
             pltpu.VMEM((seqs,) + flags_shape, jnp.int32),
-            pltpu.VMEM((seqs, rows, size), half),
-            pltpu.VMEM((seqs, text_rows, size), half),
-            pltpu.VMEM((seqs, rows, size), half),
-            pltpu.VMEM((seqs, text_rows, size), half),
+            pltpu.VMEM((seqs, rows + text_rows, size), half),
+            pltpu.VMEM((seqs, rows + text_rows, size), half),
+            pltpu.VMEM((seqs, rows + text_rows, size), half),
             pltpu.VMEM((seqs * (rows + text_rows), size), half),
             pltpu.VMEM((size, seqs * (rows + text_rows)), half),
             pltpu.VMEM((rows + text_rows, size), jnp.float32),
             pltpu.VMEM((seqs, sections, rows // sections, size), half),
             pltpu.VMEM((seqs, text_rows, size), half),
-            dma((7, heads)),
-            dma((7, seqs)),
+            pltpu.VMEM((rows + text_rows, width), half),
+            pltpu.VMEM((rows + text_rows, width), half),
+            pltpu.VMEM((rows + text_rows, width), half),
+            dma((4, heads)),
+            dma((4, seqs)),
             dma((seqs, sections)),
             dma((seqs,)),
             dma((sections * heads,)),
             dma((heads,)),
+            pltpu.SemaphoreType.REGULAR,
+            dma((6,)),
         ],
         compiler_params=pltpu.CompilerParams(
             collective_id=0, has_side_effects=True, vmem_limit_bytes=60 * 1024 * 1024

time: 38.2 us -> 37 us (0.969)
  Pallas kernels: 35.1 us -> 33.9 us
    pallas_call x1, Pallas kernels: 35.1 us -> 33.9 us  [by_heads(): pl.pallas_call(functools.partial(head_kernel, heads, seqs, sections), out...]
where the time goes in v3:
time: 37 us; the launch traced here: 36.8 us
  Pallas kernels  33.9 us (92%)
  local copies, waits for them, and re-layouts  2.25 us (6%)
  between operations  0.65 us (2%)
    pallas_call x1, Pallas kernels, by_heads(): pl.pallas_call(functools.partial(head_kernel, heads, seqs, sections), out...  33.9 us
    unnamed x4, local copies, waits for them, and re-layouts  2.25 us

profile of v3, /device:TPU:0, one launch (start us, length us, event | category | flops | bytes accessed | tf_op | source)
XLA Modules:
  0.0 36.8 jit_solution(707084154636243263)
XLA Ops:
  0.6 33.9 %shard_map.95 = (bf16[32,3072]{1,0:T(8,128)(2,1)}, bf16[32,768]{1,0:T(8,128)(2,1)}) custom-call(bf16[128,768]{1,0:T(8,128)(2,1)} %q_img.1, bf16[128,768]{1,0:T(8,128)(2,1)} %k_img.1, bf16[128,768]{1,0:T(8,128)(2,1)} %v_img.1, bf16[32,768]{1,0:T(8,128)(2,1)} %q_txt.1, bf16[32,768]{1,0:T(8,128)(2,1)} %k_txt.1, bf16[32,768]{1,0:T(8,128)(2,1)} %v_txt.1, ...), custom_call_target="tpu_custom_call" | custom-call | tf_op jit(solution)/shard_map/pallas_call | solution.py:431
  34.5 0.0 copy-start
  34.6 1.6 %copy.12 = bf16[32,1,3072]{2,0,1:T(8,128)(2,1)} copy(bf16[32,1,3072]{2,0,1:T(8,128)(2,1)} %bitcast.1) | data formatting | bytes 393216
  36.2 0.0 copy-done
  36.2 0.6 %copy.13 = bf16[32,768]{1,0:T(8,128)(2,1)} copy(bf16[32,768]{1,0:T(8,128)(2,1)S(1)} %copy-done) | data formatting | bytes 98304
Async XLA Ops:
  34.5 1.6 %copy-start = (bf16[32,768]{1,0:T(8,128)(2,1)S(1)}, bf16[32,768]{1,0:T(8,128)(2,1)}, u32[]{:S(2)}) copy-start(bf16[32,768]{1,0:T(8,128)(2,1)} %get-tuple-element.9) | copy-start | bytes 147460

commit v4 on v3

--- a/solution.py
+++ b/solution.py
@@ -312,7 +312,7 @@
         lax.fori_loop(0, seqs, take_values, 0)
 
         def answer(step, carry):
-            chunk = partner(me, step, seqs)
+            chunk = partner(me, lax.rem(step + seqs // 2, seqs), seqs)
             inward(3, chunk).wait()
             queries = jnp.concatenate(
                 [scaled(q_got[chunk, :rows], 0), scaled(q_got[chunk, rows:], 2)], axis=0

time: 37 us -> 36.7 us (level)
  Pallas kernels: 33.9 us -> 33.3 us
    pallas_call x1, Pallas kernels: 33.9 us -> 33.3 us  [by_heads(): pl.pallas_call(functools.partial(head_kernel, heads, seqs, sections), out...]
where the time goes in v4:
time: 36.7 us; the launch traced here: 36.2 us
  Pallas kernels  33.3 us (91%)
  local copies, waits for them, and re-layouts  2.25 us (6%)
  between operations  0.65 us (2%)
    pallas_call x1, Pallas kernels, by_heads(): pl.pallas_call(functools.partial(head_kernel, heads, seqs, sections), out...  33.3 us
    unnamed x4, local copies, waits for them, and re-layouts  2.25 us

profile of v4, /device:TPU:0, one launch (start us, length us, event | category | flops | bytes accessed | tf_op | source)
XLA Modules:
  0.0 36.2 jit_solution(6267012135489509)
XLA Ops:
  0.6 33.3 %shard_map.95 = (bf16[32,3072]{1,0:T(8,128)(2,1)}, bf16[32,768]{1,0:T(8,128)(2,1)}) custom-call(bf16[128,768]{1,0:T(8,128)(2,1)} %q_img.1, bf16[128,768]{1,0:T(8,128)(2,1)} %k_img.1, bf16[128,768]{1,0:T(8,128)(2,1)} %v_img.1, bf16[32,768]{1,0:T(8,128)(2,1)} %q_txt.1, bf16[32,768]{1,0:T(8,128)(2,1)} %k_txt.1, bf16[32,768]{1,0:T(8,128)(2,1)} %v_txt.1, ...), custom_call_target="tpu_custom_call" | custom-call | tf_op jit(solution)/shard_map/pallas_call | solution.py:431
  33.9 0.0 copy-start
  34.0 1.6 %copy.12 = bf16[32,1,3072]{2,0,1:T(8,128)(2,1)} copy(bf16[32,1,3072]{2,0,1:T(8,128)(2,1)} %bitcast.1) | data formatting | bytes 393216
  35.6 0.0 copy-done
  35.6 0.6 %copy.13 = bf16[32,768]{1,0:T(8,128)(2,1)} copy(bf16[32,768]{1,0:T(8,128)(2,1)S(1)} %copy-done) | data formatting | bytes 98304
Async XLA Ops:
  33.9 1.6 %copy-start = (bf16[32,768]{1,0:T(8,128)(2,1)S(1)}, bf16[32,768]{1,0:T(8,128)(2,1)}, u32[]{:S(2)}) copy-start(bf16[32,768]{1,0:T(8,128)(2,1)} %get-tuple-element.9) | copy-start | bytes 147460

commit v5 on v4

--- a/solution.py
+++ b/solution.py
@@ -261,7 +261,7 @@
             src_ref=source,
             dst_ref=target,
             send_sem=image_sent.at[chunk, to_section],
-            recv_sem=image_recv.at[section * heads + my_head],
+            recv_sem=image_recv.at[0],
             device_id={"section": to_section, "seq": chunk},
             device_id_type=pl.DeviceIdType.MESH,
         )
@@ -278,7 +278,7 @@
             src_ref=source,
             dst_ref=target,
             send_sem=text_sent.at[chunk],
-            recv_sem=text_recv.at[my_head],
+            recv_sem=text_recv.at[0],
             device_id={"seq": chunk},
             device_id_type=pl.DeviceIdType.MESH,
         )
@@ -357,7 +357,7 @@
                 def _():
                     source, target = image_copy(chunk, to_section)
                     pltpu.make_async_copy(
-                        source, target, image_recv.at[section * heads + my_head]
+                        source, target, image_recv.at[0]
                     ).start()
 
             @pl.when(chunk != me)
@@ -367,7 +367,7 @@
             @pl.when(chunk == me)
             def _():
                 source, target = text_copy(chunk)
-                pltpu.make_async_copy(source, target, text_recv.at[my_head]).start()
+                pltpu.make_async_copy(source, target, text_recv.at[0]).start()
 
             return carry
 
@@ -402,19 +402,8 @@
 
         lax.fori_loop(0, seqs, sent, 0)
 
-    def arrived(head, carry):
-        place = image_out.at[:, pl.ds(pl.multiple_of(head * size, size), size)]
-        pltpu.make_async_copy(place, place, image_recv.at[head]).wait()
-        return carry
-
-    lax.fori_loop(0, sections * heads, arrived, 0)
-
-    def text_arrived(head, carry):
-        place = text_out.at[:, pl.ds(pl.multiple_of(head * size, size), size)]
-        pltpu.make_async_copy(place, place, text_recv.at[head]).wait()
-        return carry
-
-    lax.fori_loop(0, heads, text_arrived, 0)
+    pltpu.make_async_copy(image_out, image_out, image_recv.at[0]).wait()
+    pltpu.make_async_copy(text_out, text_out, text_recv.at[0]).wait()
 
 
 def by_heads(q_img, k_img, v_img, q_txt, k_txt, v_txt, norm_gains, block_map):
@@ -455,8 +444,8 @@
             dma((4, seqs)),
             dma((seqs, sections)),
             dma((seqs,)),
-            dma((sections * heads,)),
-            dma((heads,)),
+            dma((1,)),
+            dma((1,)),
             pltpu.SemaphoreType.REGULAR,
             dma((6,)),
         ],

time: 36.7 us -> 36.3 us (0.989)
  no operation moved by 1% of the time
where the time goes in v5:
time: 36.3 us; the launch traced here: 35.9 us
  Pallas kernels  33 us (91%)
  local copies, waits for them, and re-layouts  2.25 us (6%)
  between operations  0.65 us (2%)
    pallas_call x1, Pallas kernels, by_heads(): pl.pallas_call(functools.partial(head_kernel, heads, seqs, sections), out...  33 us
    unnamed x4, local copies, waits for them, and re-layouts  2.25 us

profile of v5, /device:TPU:0, one launch (start us, length us, event | category | flops | bytes accessed | tf_op | source)
XLA Modules:
  0.0 35.9 jit_solution(1227167743845841524)
XLA Ops:
  0.6 33.0 %shard_map.95 = (bf16[32,3072]{1,0:T(8,128)(2,1)}, bf16[32,768]{1,0:T(8,128)(2,1)}) custom-call(bf16[128,768]{1,0:T(8,128)(2,1)} %q_img.1, bf16[128,768]{1,0:T(8,128)(2,1)} %k_img.1, bf16[128,768]{1,0:T(8,128)(2,1)} %v_img.1, bf16[32,768]{1,0:T(8,128)(2,1)} %q_txt.1, bf16[32,768]{1,0:T(8,128)(2,1)} %k_txt.1, bf16[32,768]{1,0:T(8,128)(2,1)} %v_txt.1, ...), custom_call_target="tpu_custom_call" | custom-call | tf_op jit(solution)/shard_map/pallas_call | solution.py:420
  33.6 0.0 copy-start
  33.6 1.6 %copy.12 = bf16[32,1,3072]{2,0,1:T(8,128)(2,1)} copy(bf16[32,1,3072]{2,0,1:T(8,128)(2,1)} %bitcast.1) | data formatting | bytes 393216
  35.3 0.0 copy-done
  35.3 0.6 %copy.13 = bf16[32,768]{1,0:T(8,128)(2,1)} copy(bf16[32,768]{1,0:T(8,128)(2,1)S(1)} %copy-done) | data formatting | bytes 98304
Async XLA Ops:
  33.6 1.6 %copy-start = (bf16[32,768]{1,0:T(8,128)(2,1)S(1)}, bf16[32,768]{1,0:T(8,128)(2,1)}, u32[]{:S(2)}) copy-start(bf16[32,768]{1,0:T(8,128)(2,1)} %get-tuple-element.9) | copy-start | bytes 147460
